TPU v7x, 256 devices: a whole 4x4x8 slice. The times are simulated.
256 devices in a mesh: frame: 32 (over x, z_hi, core), pix: 8 (over z_lo, y).
Axes of the slice: x: 4, y: 4, z: 8 (z_hi: 4, z_lo: 2; z = z_hi * 2 + z_lo), core: 2. Of those that a mesh axis runs over, the one named last changes fastest.
Arguments:
- frames: float32 [16384, 16384], P('frame', 'pix'), may hold values from 2 to 42, as said below
- dark: float32 [16384], P('pix'), may hold values from 0.5 to 1.9
Outputs:
- two_time: float32 [512, 32, 8, 512], P('pix', 'frame')
Inputs may be any that keep to these rules, and one draw needn't show every extreme that they name: `frames`: every frame count exceeds every dark level by a positive signal.
All inputs are finite; a program needn't handle non-finite values.
Results may differ from a plain program's by a relative error of at most 0.0003.
Values may be sent and summed in bfloat16 or wider, within the bound.
A program may use at most 128 MiB of HBM per device.

v0:
```python
import jax
import jax.numpy as jnp
from jax import lax
from jax.sharding import PartitionSpec as P

BS = 512
BAND = 8


def from_behind(block, axis, distance):
    devices = range(lax.axis_size(axis))
    route = [(i - distance, i) for i in devices if i - distance in devices]
    return lax.ppermute(block, axis, route)


def on_device(frames, dark):
    signal = frames - dark[None, :]
    local_rows = frames.shape[0]
    total_frames = local_rows * lax.axis_size("frame")
    pixel_mean = lax.psum(jnp.sum(signal, axis=0), "frame") / total_frames
    normalized = (signal / pixel_mean[None, :]).astype(jnp.bfloat16)
    local_blocks = local_rows // BS
    reach_count = (BAND + local_blocks - 2) // local_blocks
    pieces = [normalized]
    current = normalized
    for offset in range(reach_count):
        current = from_behind(current, "frame", -1)
        pieces.append(current)
    extended = jnp.concatenate(pieces, axis=0)
    pix_total = normalized.shape[1] * lax.axis_size("pix")
    ext_mean = lax.psum(jnp.sum(extended, axis=1, dtype=jnp.float32), "pix") / pix_total
    own_rows = BS // lax.axis_size("pix")
    product = lax.dot_general(
        normalized, extended, (((1,), (1,)), ((), ())), preferred_element_type=jnp.float32
    )
    products_list = [product.reshape(lax.axis_size("pix") * own_rows, BAND, BS)]
    gram_sums = lax.psum_scatter(
        jnp.stack(products_list, axis=1), "pix", scatter_dimension=0, tiled=True
    )
    row_share = gram_sums.shape[0]
    first_own = lax.axis_index("pix") * row_share
    own_mean = ext_mean[:local_rows].reshape(local_blocks, BS)
    left_mean = jnp.transpose(lax.dynamic_slice_in_dim(own_mean, first_own, row_share, 1))
    right_mean = jnp.stack([ext_mean.reshape(BAND, BS)], axis=0)
    global_block = (
        lax.axis_index("frame") * local_blocks
        + jnp.arange(local_blocks, dtype=jnp.int32)[:, None]
        + jnp.arange(BAND, dtype=jnp.int32)[None, :]
    )
    in_band = global_block < local_blocks * lax.axis_size("frame")
    safe_right = jnp.where(in_band[:, :, None], right_mean, jnp.ones_like(right_mean))
    result = gram_sums / (pix_total * left_mean[:, :, None, None] * safe_right[None, :, :, :])
    return jnp.where(in_band[None, :, :, None], result, jnp.zeros_like(result))


def solution(mesh):
    placed = (P("frame", "pix"), P("pix"))
    return jax.shard_map(
        on_device,
        mesh=mesh,
        in_specs=placed,
        out_specs=P("pix", "frame", None, None),
        check_vma=False,
    )
```

profile of v0, /device:TPU:1, one launch (start us, length us, event | category | flops | bytes accessed | tf_op | source)
XLA Modules:
  0.0 570.8 jit_solution(5852615752855470511)
XLA Ops:
  6.5 2.6 subtract_reduce_fusion
  9.1 74.4 %psum.14 = f32[2048]{0:T(1024)S(1)} all-reduce(f32[2048]{0:T(1024)S(1)} %subtract_reduce_fusion), channel_id=1, replica_groups=mesh['frame'=32,'pix'=8] {'frame'}, use_global_device_ids=true, to_apply=%region_1.0 | all-reduce | flops 2048 | bytes 16384 | tf_op jit(solution)/shard_map/psum | solution.py:20
  83.5 4.2 constant_dynamic-update-slice_fusion.7
  87.6 7.9 %collective-permute-start = (bf16[512,2048]{1,0:T(8,128)(2,1)S(1)}, bf16[512,2048]{1,0:T(8,128)(2,1)S(1)}, u32[]{:S(2)}, u32[]{:S(2)}) collective-permute-start(bf16[512,2048]{1,0:T(8,128)(2,1)S(1)} %get-tuple-element.6), channel_id=1, source_target_pairs={{8,0},{16,8},{24,16},{32,24},{40,32},{48,40},{56,48},{64,56},{72,6... | collective-permute-start | bytes 6291464 | tf_op jit(solution)/shard_map/ppermute | solution.py:13
  95.5 45.6 %collective-permute-done = bf16[512,2048]{1,0:T(8,128)(2,1)S(1)} collective-permute-done((bf16[512,2048]{1,0:T(8,128)(2,1)S(1)}, bf16[512,2048]{1,0:T(8,128)(2,1)S(1)}, u32[]{:S(2)}, u32[]{:S(2)}) %collective-permute-start) | collective-permute-done | bytes 2097184 | tf_op jit(solution)/shard_map/ppermute | solution.py:13
  141.1 1.9 collective-permute-start.1
  143.0 50.1 %collective-permute-done.1 = bf16[512,2048]{1,0:T(8,128)(2,1)S(1)} collective-permute-done((bf16[512,2048]{1,0:T(8,128)(2,1)S(1)}, bf16[512,2048]{1,0:T(8,128)(2,1)S(1)}, u32[]{:S(2)}, u32[]{:S(2)}) %collective-permute-start.1) | collective-permute-done | bytes 2097184 | tf_op jit(solution)/shard_map/ppermute | solution.py:13
  193.1 1.9 collective-permute-start.2
  195.0 48.7 %collective-permute-done.2 = bf16[512,2048]{1,0:T(8,128)(2,1)S(1)} collective-permute-done((bf16[512,2048]{1,0:T(8,128)(2,1)S(1)}, bf16[512,2048]{1,0:T(8,128)(2,1)S(1)}, u32[]{:S(2)}, u32[]{:S(2)}) %collective-permute-start.2) | collective-permute-done | bytes 2097184 | tf_op jit(solution)/shard_map/ppermute | solution.py:13
  243.7 1.9 collective-permute-start.3
  245.6 38.1 %collective-permute-done.3 = bf16[512,2048]{1,0:T(8,128)(2,1)S(1)} collective-permute-done((bf16[512,2048]{1,0:T(8,128)(2,1)S(1)}, bf16[512,2048]{1,0:T(8,128)(2,1)S(1)}, u32[]{:S(2)}, u32[]{:S(2)}) %collective-permute-start.3) | collective-permute-done | bytes 2097184 | tf_op jit(solution)/shard_map/ppermute | solution.py:13
  283.7 1.9 collective-permute-start.4
  285.6 41.5 %collective-permute-done.4 = bf16[512,2048]{1,0:T(8,128)(2,1)S(1)} collective-permute-done((bf16[512,2048]{1,0:T(8,128)(2,1)S(1)}, bf16[512,2048]{1,0:T(8,128)(2,1)S(1)}, u32[]{:S(2)}, u32[]{:S(2)}) %collective-permute-start.4) | collective-permute-done | bytes 2097184 | tf_op jit(solution)/shard_map/ppermute | solution.py:13
  327.1 1.9 collective-permute-start.5
  329.0 42.9 %collective-permute-done.5 = bf16[512,2048]{1,0:T(8,128)(2,1)S(1)} collective-permute-done((bf16[512,2048]{1,0:T(8,128)(2,1)S(1)}, bf16[512,2048]{1,0:T(8,128)(2,1)S(1)}, u32[]{:S(2)}, u32[]{:S(2)}) %collective-permute-start.5) | collective-permute-done | bytes 2097184 | tf_op jit(solution)/shard_map/ppermute | solution.py:13
  371.9 2.1 collective-permute-start.6
  378.4 1.5 constant_dynamic-update-slice_fusion.3
  382.8 34.3 %collective-permute-done.6 = bf16[512,2048]{1,0:T(8,128)(2,1)S(1)} collective-permute-done((bf16[512,2048]{1,0:T(8,128)(2,1)S(1)}, bf16[512,2048]{1,0:T(8,128)(2,1)S(1)}, u32[]{:S(2)}, u32[]{:S(2)}) %collective-permute-start.6) | collective-permute-done | bytes 2097184 | tf_op jit(solution)/shard_map/ppermute | solution.py:13
  418.6 11.7 %fusion = f32[512,4096]{1,0:T(8,128)S(1)} fusion(bf16[512,2048]{1,0:T(8,128)(2,1)S(1)} %get-tuple-element.6, bf16[4096,2048]{1,0:T(8,128)(2,1)} %constant_dynamic-update-slice_fusion), kind=kOutput, calls=%fused_computation.17 | convolution fusion | flops 8589934592 | bytes 27262976 | tf_op jit(solution)/shard_map/dot_general | solution.py:33
  430.3 11.3 %copy.4 = f32[64,8,8,512]{3,2,1,0:T(8,128)} copy(f32[64,8,8,512]{3,1,2,0:T(8,128)S(1)} %bitcast.9) | data formatting | bytes 16777216
  441.7 6.8 %convert_reduce_fusion = f32[4096]{0:T(1024)S(1)} fusion(bf16[4096,2048]{1,0:T(8,128)(2,1)} %constant_dynamic-update-slice_fusion), kind=kLoop, calls=%fused_computation | loop fusion | flops 16773120 | bytes 16793600 | tf_op jit(solution)/shard_map/reduce_sum | solution.py:31
  448.5 45.8 %psum.15 = f32[4096]{0:T(1024)S(1)} all-reduce(f32[4096]{0:T(1024)S(1)} %convert_reduce_fusion), channel_id=1, replica_groups=mesh['frame'=32,'pix'=8] {'pix'}, use_global_device_ids=true, to_apply=%region_4.0 | all-reduce | flops 4096 | bytes 32768 | tf_op jit(solution)/shard_map/psum | solution.py:31
  494.5 67.1 %reduce-scatter.2.cloned.1.call-done = f32[64,1,8,512]{3,2,1,0:T(8,128)} async-done(((f32[512,1,8,512]{3,2,1,0:T(8,128)}), f32[64,1,8,512]{3,2,1,0:T(8,128)}) %reduce-scatter.2.cloned.1.call-update) | async-done | bytes 1048592 | tf_op jit(solution)/shard_map/reduce_scatter | solution.py:37
  561.6 2.4 divide_select_fusion
  (15 shorter events, 9.0 us)
Async XLA Ops:
  6.5 555.0 %reduce-scatter.2.cloned.1.call-start = ((), (), s32[]{:S(2)}) async-start(), calls=%async_computation.1 | async-start | bytes 9437184 | tf_op jit(solution)/shard_map/reduce_scatter | solution.py:37
  87.6 53.4 %collective-permute-start = (bf16[512,2048]{1,0:T(8,128)(2,1)S(1)}, bf16[512,2048]{1,0:T(8,128)(2,1)S(1)}, u32[]{:S(2)}, u32[]{:S(2)}) collective-permute-start(bf16[512,2048]{1,0:T(8,128)(2,1)S(1)} %get-tuple-element.6), channel_id=1, source_target_pairs={{8,0},{16,8},{24,16},{32,24},{40,32},{48,40},{56,48},{64,56},{72,6... | collective-permute-start | bytes 6291464 | tf_op jit(solution)/shard_map/ppermute | solution.py:13
  141.1 52.0 %collective-permute-start.1 = (bf16[512,2048]{1,0:T(8,128)(2,1)S(1)}, bf16[512,2048]{1,0:T(8,128)(2,1)S(1)}, u32[]{:S(2)}, u32[]{:S(2)}) collective-permute-start(bf16[512,2048]{1,0:T(8,128)(2,1)S(1)} %collective-permute-done), channel_id=1, source_target_pairs={{8,0},{16,8},{24,16},{32,24},{40,32},{48,40},{56,48},{64,56},{72,6... | collective-permute-start | bytes 6291464 | tf_op jit(solution)/shard_map/ppermute | solution.py:13
  193.1 50.6 %collective-permute-start.2 = (bf16[512,2048]{1,0:T(8,128)(2,1)S(1)}, bf16[512,2048]{1,0:T(8,128)(2,1)S(1)}, u32[]{:S(2)}, u32[]{:S(2)}) collective-permute-start(bf16[512,2048]{1,0:T(8,128)(2,1)S(1)} %collective-permute-done.1), channel_id=1, source_target_pairs={{8,0},{16,8},{24,16},{32,24},{40,32},{48,40},{56,48},{64,56},{72,6... | collective-permute-start | bytes 6291464 | tf_op jit(solution)/shard_map/ppermute | solution.py:13
  243.7 40.0 %collective-permute-start.3 = (bf16[512,2048]{1,0:T(8,128)(2,1)S(1)}, bf16[512,2048]{1,0:T(8,128)(2,1)S(1)}, u32[]{:S(2)}, u32[]{:S(2)}) collective-permute-start(bf16[512,2048]{1,0:T(8,128)(2,1)S(1)} %collective-permute-done.2), channel_id=1, source_target_pairs={{8,0},{16,8},{24,16},{32,24},{40,32},{48,40},{56,48},{64,56},{72,6... | collective-permute-start | bytes 6291464 | tf_op jit(solution)/shard_map/ppermute | solution.py:13
  283.7 43.4 %collective-permute-start.4 = (bf16[512,2048]{1,0:T(8,128)(2,1)S(1)}, bf16[512,2048]{1,0:T(8,128)(2,1)S(1)}, u32[]{:S(2)}, u32[]{:S(2)}) collective-permute-start(bf16[512,2048]{1,0:T(8,128)(2,1)S(1)} %collective-permute-done.3), channel_id=1, source_target_pairs={{8,0},{16,8},{24,16},{32,24},{40,32},{48,40},{56,48},{64,56},{72,6... | collective-permute-start | bytes 6291464 | tf_op jit(solution)/shard_map/ppermute | solution.py:13
  327.1 44.8 %collective-permute-start.5 = (bf16[512,2048]{1,0:T(8,128)(2,1)S(1)}, bf16[512,2048]{1,0:T(8,128)(2,1)S(1)}, u32[]{:S(2)}, u32[]{:S(2)}) collective-permute-start(bf16[512,2048]{1,0:T(8,128)(2,1)S(1)} %collective-permute-done.4), channel_id=1, source_target_pairs={{8,0},{16,8},{24,16},{32,24},{40,32},{48,40},{56,48},{64,56},{72,6... | collective-permute-start | bytes 6291464 | tf_op jit(solution)/shard_map/ppermute | solution.py:13
  371.9 45.2 %collective-permute-start.6 = (bf16[512,2048]{1,0:T(8,128)(2,1)S(1)}, bf16[512,2048]{1,0:T(8,128)(2,1)S(1)}, u32[]{:S(2)}, u32[]{:S(2)}) collective-permute-start(bf16[512,2048]{1,0:T(8,128)(2,1)S(1)} %collective-permute-done.5), channel_id=1, source_target_pairs={{8,0},{16,8},{24,16},{32,24},{40,32},{48,40},{56,48},{64,56},{72,6... | collective-permute-start | bytes 6291464 | tf_op jit(solution)/shard_map/ppermute | solution.py:13
Sparse Core Ops, SparseCore 0:
  441.8 119.7 reduce-scatter.1
where the time goes:
time: 571 us
  waiting for transfers between devices  368 us (64%)
  blocking collectives  120 us (21%)
  local copies, waits for them, and re-layouts  21.6 us (4%)
  starting transfers between devices  19.5 us (3%)
  other arithmetic  16.1 us (3%)
  between operations  13.5 us (2%)
  matrix products  11.7 us (2%)
    ppermute x7, waiting for transfers between devices, from_behind(): return lax.ppermute(block, axis, route)  301 us
    psum x1, blocking collectives, on_device(): pixel_mean = lax.psum(jnp.sum(signal, axis=0), 'frame') / total_frames  74.4 us
    reduce_scatter x1, waiting for transfers between devices, on_device(): lax.psum_scatter(jnp.stack(products_list, axis=1), 'pix', scatter_dimensi...  67.1 us
    psum x1, blocking collectives, on_device(): lax.psum(jnp.sum(extended, axis=1, dtype=jnp.float32), 'pix') / pix_total  45.8 us
    unnamed x7, local copies, waits for them, and re-layouts  20.2 us
    ppermute x7, starting transfers between devices, from_behind(): return lax.ppermute(block, axis, route)  19.5 us
    dot_general x1, matrix products, on_device(): lax.dot_general(normalized, extended, (((1,), (1,)), ((), ())), preferred...  11.7 us
  transfers between devices with their start and end apart: 8, of which 8 were waited for; matrix products, arithmetic and copies ran while one was open for 3% of the time, Pallas kernels for 0%

commit v1 on v0

v1 whole, which is shorter than its diff:
```python
import functools

import jax
import jax.numpy as jnp
from jax import lax
from jax.experimental import pallas as pl
from jax.experimental.pallas import tpu as pltpu
from jax.sharding import PartitionSpec as P

BS = 512
CR = 128
T = BS // CR
BAND = 8
F32 = jnp.float32
BF16 = jnp.bfloat16
MESH = pl.DeviceIdType.MESH


def nt_dot(left, right):
    return lax.dot_general(left, right, (((1,), (1,)), ((), ())), preferred_element_type=F32)


def kernel(total_frames, total_pix, frames, dark, out,
           fr, a, aw, ap, nx, th, ex, nw, ys, yr, zs, zo, zr, shs, shr,
           cs, cr, winv, fs, fy, fz, fmr, fcol,
           fl_s, x_s, x_r, dn_s, dn_r, up_s, up_r, ce_s, ce_r, cn_s, cn_r, ct_s, ct_r,
           ys_s, ys_r, zs_s, zs_r, sh_s, sh_r, cs_s, cs_r, fy_s, fy_r, fz_s, fz_r, fm_s, fm_r):
    f = lax.axis_index("frame")
    p = lax.axis_index("pix")
    nf = 32
    c = lax.rem(f, 2)
    k = f // 2
    z = lax.rem(k, 4)
    x = k // 4
    y = lax.rem(p, 4)
    zl = p // 4

    def fdev(nx_, nz_, nc_):
        return ((nx_ * 4 + nz_) * 2 + nc_, p)

    def fwrap(d):
        return (lax.rem(f + d + nf, nf), p)

    def zdev(o):
        return fdev(x, lax.rem(z + o, 4), c)

    def xdev(o):
        return fdev(lax.rem(x + o, 4), z, c)

    def ydev(o):
        return (f, zl * 4 + lax.rem(y + o, 4))

    core = fdev(x, z, 1 - c)
    zpartner = (f, (1 - zl) * 4 + y)

    barrier = pltpu.get_barrier_semaphore()
    greet = [core, zpartner]
    greet += [zdev(o) for o in (1, 2, 3)]
    greet += [xdev(o) for o in (1, 2, 3)]
    greet += [ydev(o) for o in (1, 2, 3)]
    greet += [fwrap(d) for d in range(1, 8)]
    greet += [fwrap(-2)]
    for g in greet:
        pl.semaphore_signal(barrier, inc=1, device_id=g, device_id_type=MESH)

    def rows(t):
        return pl.ds(t * CR, CR)

    loads = [pltpu.make_async_copy(frames.at[rows(t)], fr.at[rows(t)], fl_s.at[t]) for t in range(T)]
    for ld in loads:
        ld.start()

    def remote(src, dst, s, r, dev):
        return pltpu.make_async_remote_copy(
            src_ref=src, dst_ref=dst, send_sem=s, recv_sem=r, device_id=dev, device_id_type=MESH)

    def x_copy(t):
        return remote(a.at[rows(t)], ap.at[rows(t)], x_s.at[t], x_r.at[t], xdev(3))

    def dn_copy(t, src):
        return remote(src.at[rows(t)], nx.at[t, c], dn_s.at[t], dn_r.at[t], zdev(3))

    def up_copy(t, src):
        return remote(src.at[rows(t)], th.at[t, c], up_s.at[t], up_r.at[t], zdev(1))

    def ce_copy(t, src):
        return remote(src.at[rows(t)], ex.at[rows(t)], ce_s.at[t], ce_r.at[t], core)

    def cn_copy(t):
        return remote(nx.at[t, c], nx.at[t, c], cn_s.at[t], cn_r.at[t], core)

    def ct_copy(t):
        return remote(th.at[t, c], th.at[t, c], ct_s.at[t], ct_r.at[t], core)

    def cn_arrive(t):
        return remote(nx.at[t, 1 - c], nx.at[t, 1 - c], cn_s.at[t], cn_r.at[t], core)

    def ct_arrive(t):
        return remote(th.at[t, 1 - c], th.at[t, 1 - c], ct_s.at[t], ct_r.at[t], core)

    dk = dark[0:1, :]
    colsum = None
    for t in range(T):
        loads[t].wait()
        sig = fr[t * CR:(t + 1) * CR, :] - dk
        a[t * CR:(t + 1) * CR, :] = sig.astype(BF16)
        part = jnp.sum(sig, axis=0, keepdims=True)
        colsum = part if colsum is None else colsum + part
        if t == 0:
            pl.semaphore_wait(barrier, len(greet))
        x_copy(t).start()

        @pl.when(z >= 1)
        def _():
            dn_copy(t, a).start()

        @pl.when(z == 3)
        def _():
            up_copy(t, a).start()

        @pl.when(c == 1)
        def _():
            ce_copy(t, a).start()

    width = colsum.shape[1] // 8
    for i in range(8):
        cs[0, i:i + 1, :] = colsum[:, i * width:(i + 1) * width]

    def cs_copy(stage, i, dev):
        return remote(cs.at[stage], cr.at[i], cs_s.at[i], cs_r.at[i], dev)

    cs_copies = [cs_copy(0, 0, core)]
    cs_copies += [cs_copy(1, o, zdev(o)) for o in (1, 2, 3)]
    cs_copies += [cs_copy(2, 3 + o, xdev(o)) for o in (1, 2, 3)]
    cs_copies[0].start()
    cs_copies[0].wait_recv()
    cs[1] = cs[0] + cr[0]
    for i in (1, 2, 3):
        cs_copies[i].start()
    for i in (1, 2, 3):
        cs_copies[i].wait_recv()
    cs[2] = (cs[1] + cr[1]) + (cr[2] + cr[3])
    for i in (4, 5, 6):
        cs_copies[i].start()
    for i in (4, 5, 6):
        cs_copies[i].wait_recv()
    pixel_mean = ((cs[2] + cr[4]) + (cr[5] + cr[6])) / total_frames
    inv8 = 1.0 / pixel_mean
    for i in range(8):
        winv[0:1, i * width:(i + 1) * width] = inv8[i:i + 1, :]

    def arrive_ap(t):
        x_copy(t).wait_recv()

        @pl.when(z == 0)
        def _():
            dn_copy(t, ap).start()

        @pl.when(z <= 2)
        def _():
            up_copy(t, ap).start()

        @pl.when(c == 0)
        def _():
            ce_copy(t, ap).start()

    def arrive_nx(t):
        dn_copy(t, a).wait_recv()
        cn_copy(t).start()

    def arrive_th(t):
        up_copy(t, a).wait_recv()
        ct_copy(t).start()

    def y_copy(m, s0, ns, c0, nc, o):
        dst = lax.rem(y + o, 4)
        return remote(
            ys.at[pl.ds(s0, ns), :, pl.ds(pl.multiple_of(dst * 64, 64), 64), pl.ds(c0, nc)],
            yr.at[o - 1, pl.ds(s0, ns), :, :, pl.ds(c0, nc)],
            ys_s.at[m, o - 1], ys_r.at[m, o - 1], ydev(o))

    def z_copy(m, s0, ns, c0, nc):
        return remote(zs.at[pl.ds(s0, ns), :, pl.ds(c0, nc)], zr.at[pl.ds(s0, ns), :, pl.ds(c0, nc)],
                      zs_s.at[m], zs_r.at[m], zpartner)

    def sh_copy(m, c0, nc):
        return remote(shs.at[:, :, pl.ds(c0, nc)], shr.at[:, :, pl.ds(c0, nc)],
                      sh_s.at[m], sh_r.at[m], fwrap(2))

    messages = [(0, 0, 1, 0, BS), (1, 1, 1, 0, BS)]
    messages += [(2 + t, 2, 2, t * CR, CR) for t in range(T)]
    messages += [(2 + T + t, 4, 2, t * CR, CR) for t in range(T)]
    messages += [(2 + 2 * T + t, 6, 2, t * CR, CR) for t in range(T)]

    def y_start(m):
        for o in (2, 1, 3):
            y_copy(*messages[m], o).start()

    def z_start(m):
        _, s0, ns, c0, nc = messages[m]
        for o in (1, 2, 3):
            y_copy(*messages[m], o).wait_recv()
        mine = pl.ds(pl.multiple_of(y * 64, 64), 64)
        cols = pl.ds(c0, nc)

        def total(s, h):
            return (ys[s, h, mine, cols] + yr[0, s, h, :, cols]) + (yr[1, s, h, :, cols] + yr[2, s, h, :, cols])

        for s in range(s0, s0 + ns):
            zs[s, :, cols] = total(s, 1 - zl)
        z_copy(*messages[m]).start()
        for s in range(s0, s0 + ns):
            zo[s, :, cols] = total(s, zl)

    def z_end(m):
        _, s0, ns, c0, nc = messages[m]
        cols = pl.ds(c0, nc)
        z_copy(*messages[m]).wait_recv()
        for s in range(s0, s0 + ns):
            v = zo[s, :, cols] + zr[s, :, cols]
            if s0 == 6:
                shs[s - 6, :, cols] = v
            else:
                zo[s, :, cols] = v
        if s0 == 6:
            sh_copy(m - 2 - 2 * T, c0, nc).start()

    def pair_product(left, right, s0, t):
        for h in range(2):
            prod = nt_dot(left[h * 256:(h + 1) * 256, :], right[t].reshape(2 * CR, -1))
            ys[s0, h, :, t * CR:(t + 1) * CR] = prod[:, :CR]
            ys[s0 + 1, h, :, t * CR:(t + 1) * CR] = prod[:, CR:]

    def single_product(left, right, s0):
        for h in range(2):
            for q in range(2):
                ys[s0, h, :, q * 256:(q + 1) * 256] = nt_dot(
                    left[h * 256:(h + 1) * 256, :], right[q * 256:(q + 1) * 256, :])

    def step_nx(t):
        cn_arrive(t).wait_recv()
        pair_product(aw, nx, 2, t)
        y_start(2 + t)
        w = winv[0:1, :] * winv[0:1, :]
        nw[t * CR:(t + 1) * CR, :] = (nx[t, c].astype(F32) * w).astype(BF16)

    def step_th(t):
        ct_arrive(t).wait_recv()
        pair_product(aw, th, 4, t)
        y_start(2 + T + t)

    def step_nt(t):
        pair_product(nw, th, 6, t)
        y_start(2 + 2 * T + t)

    for t in range(T):
        w = winv[0:1, :] * winv[0:1, :]
        aw[t * CR:(t + 1) * CR, :] = ((fr[t * CR:(t + 1) * CR, :] - dk) * w).astype(BF16)
    inv = winv[0:1, :]
    hi = inv.astype(BF16).astype(F32)
    row = lax.broadcasted_iota(jnp.int32, (16, inv.shape[1]), 0)
    mix = jnp.where(row == 0, hi, jnp.where(row == 1, inv - hi, 0.0)).astype(BF16)
    fsum = jnp.sum(nt_dot(mix, a[...]), axis=0, keepdims=True)
    fs[0] = jnp.broadcast_to(fsum, (8, BS))

    def fy_copy(o):
        return remote(fs.at[0], fy.at[o - 1], fy_s.at[o - 1], fy_r.at[o - 1], ydev(o))

    fz_copy = remote(fs.at[1], fz, fz_s.at[0], fz_r.at[0], zpartner)

    def fm_copy(d):
        return remote(fmr.at[0], fmr.at[d], fm_s.at[d], fm_r.at[d], fwrap(-d))

    for o in (1, 2, 3):
        fy_copy(o).start()

    arrive_ap(0)
    single_product(aw, a, 0)
    y_start(0)

    for o in (1, 2, 3):
        fy_copy(o).wait_recv()
    fs[1] = (fs[0] + fy[0]) + (fy[1] + fy[2])
    fz_copy.start()
    fz_copy.wait_recv()
    fmr[0] = (fs[1] + fz[...]) / total_pix
    for d in range(1, BAND):
        fm_copy(d).start()

    arrive_ap(1)
    arrive_nx(0)
    arrive_ap(2)
    step_nx(0)
    arrive_th(0)
    z_start(0)
    arrive_ap(3)
    step_th(0)
    arrive_nx(1)
    for t in range(T):
        ce_copy(t, a).wait_recv()
    single_product(aw, ex, 1)
    y_start(1)
    z_end(0)
    z_start(2)
    step_nx(1)
    arrive_th(1)
    z_end(2)
    z_start(1)
    z_start(2 + T)
    step_th(1)
    arrive_nx(2)
    z_end(1)
    z_end(2 + T)
    z_start(3)
    step_nx(2)
    arrive_th(2)
    z_end(3)
    z_start(3 + T)
    step_th(2)
    arrive_nx(3)
    z_end(3 + T)
    z_start(4)
    z_start(4 + T)
    step_nx(3)
    for t in range(3):
        step_nt(t)
    z_end(4)
    z_end(4 + T)
    arrive_th(3)
    z_start(5)
    for t in range(3):
        z_start(2 + 2 * T + t)
    step_th(3)
    step_nt(3)
    z_end(5)
    for t in range(3):
        z_end(2 + 2 * T + t)
    z_start(5 + T)
    z_start(5 + 2 * T)
    z_end(5 + 2 * T)
    z_end(5 + T)

    for d in range(1, BAND):
        fm_copy(d).wait_recv()
    fcol[...] = jnp.transpose(jnp.broadcast_to(fmr[0, 0:1, :], (128, BS)))
    left = 1.0 / (fcol[pl.ds(pl.multiple_of(p * 64, 64), 64), :] * total_pix)
    left = jnp.concatenate([left] * (BS // 128), axis=1)
    for t in range(T):
        sh_copy(t, t * CR, CR).wait_recv()

    def finish(order):
        for lag in range(BAND):
            s = order[lag]
            v = shr[s - 6] if s >= 6 else zo[s]
            v = v * left * (1.0 / fmr[lag, 0:1, :])
            out[:, lag, :] = jnp.where(f + lag < nf, v, 0.0)

    @pl.when(c == 0)
    def _():
        finish((0, 1, 2, 3, 6, 7, 4, 5))

    @pl.when(c == 1)
    def _():
        finish((0, 2, 3, 6, 7, 4, 5, 1))

    for t in range(T):
        x_copy(t).wait_send()
        dn_copy(t, a).wait_send()
        up_copy(t, a).wait_send()
        ce_copy(t, a).wait_send()
        cn_copy(t).wait_send()
        ct_copy(t).wait_send()
        sh_copy(t, t * CR, CR).wait_send()
    for copy in cs_copies:
        copy.wait_send()
    for o in (1, 2, 3):
        fy_copy(o).wait_send()
    fz_copy.wait_send()
    for d in range(1, BAND):
        fm_copy(d).wait_send()
    for m in range(len(messages)):
        for o in (1, 2, 3):
            y_copy(*messages[m], o).wait_send()
        z_copy(*messages[m]).wait_send()


def on_device(frames, dark):
    n, pix = frames.shape
    total_frames = n * lax.axis_size("frame")
    total_pix = pix * lax.axis_size("pix")
    nm = 2 + 3 * T
    dma = pltpu.SemaphoreType.DMA
    vm = pltpu.VMEM
    out = pl.pallas_call(
        functools.partial(kernel, float(total_frames), float(total_pix)),
        out_shape=jax.ShapeDtypeStruct((64, BAND, BS), F32),
        in_specs=[pl.BlockSpec(memory_space=pl.ANY), pl.BlockSpec(memory_space=pltpu.VMEM)],
        out_specs=pl.BlockSpec(memory_space=pltpu.VMEM),
        scratch_shapes=[
            vm((BS, pix), F32), vm((BS, pix), BF16), vm((BS, pix), BF16), vm((BS, pix), BF16),
            vm((T, 2, CR, pix), BF16), vm((T, 2, CR, pix), BF16), vm((BS, pix), BF16), vm((BS, pix), BF16),
            vm((8, 2, 256, BS), F32), vm((3, 8, 2, 64, BS), F32),
            vm((8, 64, BS), F32), vm((8, 64, BS), F32), vm((8, 64, BS), F32),
            vm((2, 64, BS), F32), vm((2, 64, BS), F32),
            vm((3, 8, pix // 8), F32), vm((7, 8, pix // 8), F32), vm((8, pix), F32),
            vm((2, 8, BS), F32), vm((3, 8, BS), F32), vm((8, BS), F32), vm((BAND, 8, BS), F32), vm((BS, 128), F32),
            dma((T,)),
            dma((T,)), dma((T,)), dma((T,)), dma((T,)), dma((T,)), dma((T,)),
            dma((T,)), dma((T,)), dma((T,)), dma((T,)), dma((T,)), dma((T,)),
            dma((nm, 3)), dma((nm, 3)), dma((nm,)), dma((nm,)), dma((T,)), dma((T,)),
            dma((7,)), dma((7,)), dma((3,)), dma((3,)), dma((1,)), dma((1,)), dma((BAND,)), dma((BAND,)),
        ],
        compiler_params=pltpu.CompilerParams(
            collective_id=0, has_side_effects=True, vmem_limit_bytes=56 * 1024 * 1024),
        cost_estimate=pl.CostEstimate(flops=2 * 8 * BS * BS * pix, bytes_accessed=6 * BS * pix, transcendentals=0),
    )(frames, dark.reshape(1, pix))
    return out.reshape(64, 1, BAND, BS)


def solution(mesh):
    return jax.shard_map(
        on_device,
        mesh=mesh,
        in_specs=(P("frame", "pix"), P("pix")),
        out_specs=P("pix", "frame", None, None),
        check_vma=False,
    )
```

time: 571 us -> 278 us (0.49)
  waiting for transfers between devices: 368 us -> 0 us
  Pallas kernels: 0 us -> 274 us
  blocking collectives: 120 us -> 0 us
  starting transfers between devices: 19.5 us -> 0 us
  local copies, waits for them, and re-layouts: 21.6 us -> 2.26 us
  other arithmetic: 16.1 us -> 0 us
  between operations: 13.5 us -> 0.01 us
  matrix products: 11.7 us -> 0 us
    ppermute x7 -> x0, waiting for transfers between devices: 301 us -> none  [from_behind(): return lax.ppermute(block, axis, route)]
    pallas_call x0 -> x1, Pallas kernels: none -> 274 us  [on_device(): pl.pallas_call(functools.partial(kernel, float(total_frames), float(total...]
    psum x2 -> x0, blocking collectives: 120 us -> none  [the longest x1 74.4 us: on_device(): pixel_mean = lax.psum(jnp.sum(signal, axis=0), 'frame') / total_frames]
    reduce_scatter x1 -> x0, waiting for transfers between devices: 67.1 us -> none  [on_device(): lax.psum_scatter(jnp.stack(products_list, axis=1), 'pix', scatter_dimensi...]
    ppermute x7 -> x0, starting transfers between devices: 19.5 us -> none  [from_behind(): return lax.ppermute(block, axis, route)]
    unnamed x7 -> x1, local copies, waits for them, and re-layouts: 20.2 us -> 2.26 us
    dot_general x1 -> x0, matrix products: 11.7 us -> none  [on_device(): lax.dot_general(normalized, extended, (((1,), (1,)), ((), ())), preferred...]
    reduce_sum x2 -> x0, other arithmetic: 9.4 us -> none  [the longest x1 6.83 us: on_device(): jnp.sum(extended, axis=1, dtype=jnp.float32)]
  transfers between devices with their start and end apart: 8 -> 0, of which waited for: 8 -> 0; matrix products, arithmetic and copies ran while one was open for 3% -> 0% of each run, Pallas kernels for 0% -> 0%
where the time goes in v1:
time: 278 us; the launch traced here: 276 us
  Pallas kernels  274 us (99%)
    pallas_call x1, Pallas kernels, on_device(): pl.pallas_call(functools.partial(kernel, float(total_frames), float(total...  274 us

profile of v1, /device:TPU:1, one launch (start us, length us, event | category | flops | bytes accessed | tf_op | source)
XLA Modules:
  0.0 275.9 jit_solution(13671303767888080268)
XLA Ops:
  0.0 273.6 %shard_map.28 = f32[64,8,512]{2,1,0:T(8,128)} custom-call(f32[512,2048]{1,0:T(8,128)} %frames.1, f32[1,2048]{1,0:T(1,128)} %bitcast.5), custom_call_target="tpu_custom_call" | custom-call | flops 8589934592 | bytes 6291456 | tf_op jit(solution)/shard_map/pallas_call | solution.py:394
  273.7 2.3 copy.5

commit v2 on v0

v2 whole, which is shorter than its diff:
```python
import functools

import jax
import jax.numpy as jnp
from jax import lax
from jax.experimental import pallas as pl
from jax.experimental.pallas import tpu as pltpu
from jax.sharding import PartitionSpec as P

BS = 512
SH = 64
T = 4
CS = SH // T
CR = BS // T
BAND = 8
F32 = jnp.float32
BF16 = jnp.bfloat16
MESH = pl.DeviceIdType.MESH


def nt_dot(left, right):
    return lax.dot_general(left, right, (((1,), (1,)), ((), ())), preferred_element_type=F32)


def natural(v):
    lane = lax.broadcasted_iota(jnp.int32, (v.shape[0], CR), 1)
    groups = []
    for g in range(BS // CR):
        acc = None
        for t in range(T):
            src = v[:, t * CR:(t + 1) * CR]
            for h in range(2):
                shift = (h * SH + t * CS) - (2 * g + h) * CS
                piece = pltpu.roll(src, shift % CR, 1) if shift % CR else src
                if acc is None:
                    acc = piece
                else:
                    start = h * SH + t * CS
                    acc = jnp.where((lane >= start) & (lane < start + CS), piece, acc)
        groups.append(acc)
    return jnp.concatenate(groups, axis=1)


def kernel(total_frames, total_pix, frames, dark, out,
           fr, a, aw, ap, ex, rv, nw, lw, ys, yr, zs, zo, zr, hs, hb,
           cs, cr, winv, fs, fy, fz, fmr, fcol,
           fl_s, x_s, x_r, e_s, e_r, l_s, l_r, ce_s, ce_r, c_s, c_r,
           ys_s, ys_r, zs_s, zs_r, hs_s, hb_r, cs_s, cs_r, fy_s, fy_r, fz_s, fz_r, fm_s, fm_r):
    f = lax.axis_index("frame")
    p = lax.axis_index("pix")
    nf = 32
    pix = fr.shape[1]
    c = lax.rem(f, 2)
    k = f // 2
    z = lax.rem(k, 4)
    x = k // 4
    y = lax.rem(p, 4)
    zl = p // 4

    def fdev(nx_, nz_, nc_):
        return ((nx_ * 4 + nz_) * 2 + nc_, p)

    def kdev(d):
        return (lax.rem(k + d, 16) * 2 + c, p)

    def fwrap(d):
        return (lax.rem(f + d + nf, nf), p)

    def zdev(o):
        return fdev(x, lax.rem(z + o, 4), c)

    def xdev(o):
        return fdev(lax.rem(x + o, 4), z, c)

    def ydev(o):
        return (f, zl * 4 + lax.rem(y + o, 4))

    core = fdev(x, z, 1 - c)
    zpartner = (f, (1 - zl) * 4 + y)
    plane = [core] + [fdev(x, lax.rem(z + o, 4), cc) for o in (1, 2, 3) for cc in (c, 1 - c)]
    homes = [(lax.rem(f + 2, nf), h * 4 + y) for h in range(2)]

    barrier = pltpu.get_barrier_semaphore()
    greet = [zpartner] + plane
    greet += [xdev(o) for o in (1, 2, 3)]
    greet += [ydev(o) for o in (1, 2, 3)]
    greet += [fwrap(d) for d in range(1, 8)]
    greet += [(lax.rem(f + nf - 2, nf), h * 4 + y) for h in range(2)]
    greet += [kdev(3 - 2 * zl), kdev(1 + 2 * zl)]
    for g in greet:
        pl.semaphore_signal(barrier, inc=1, device_id=g, device_id_type=MESH)

    rows = BS // 4
    loads = [pltpu.make_async_copy(frames.at[pl.ds(q * rows, rows)], fr.at[pl.ds(q * rows, rows)], fl_s.at[q])
             for q in range(4)]
    for ld in loads:
        ld.start()

    def remote(src, dst, s, r, dev):
        return pltpu.make_async_remote_copy(
            src_ref=src, dst_ref=dst, send_sem=s, recv_sem=r, device_id=dev, device_id_type=MESH)

    def part(ref, t):
        return ref.at[:, pl.ds(t * CS, CS), :]

    def x_copy(t):
        return remote(part(a, t), part(ap, t), x_s.at[t], x_r.at[t], xdev(3))

    def e_copy(t):
        return remote(part(a, t), rv.at[0, t, c], e_s.at[t], e_r.at[t], kdev(13 + 2 * zl))

    def l_copy(t, src, dev):
        return remote(part(src, t), rv.at[1, t, c], l_s.at[t], l_r.at[t], dev)

    def ce_copy(t, src):
        return remote(part(src, t), part(ex, t), ce_s.at[t], ce_r.at[t], core)

    def c_copy(e, t):
        return remote(rv.at[e, t, c], rv.at[e, t, c], c_s.at[e, t], c_r.at[e, t], core)

    dk = dark[0:1, :]
    colsum = None
    for q in range(4):
        loads[q].wait()
        sig = fr[q * rows:(q + 1) * rows, :] - dk
        a[2 * q:2 * q + 2] = sig.astype(BF16).reshape(2, SH, pix)
        partial = jnp.sum(sig, axis=0, keepdims=True)
        colsum = partial if colsum is None else colsum + partial

    width = pix // 8
    for i in range(8):
        cs[0, i:i + 1, :] = colsum[:, i * width:(i + 1) * width]

    def cs_copy(stage, i, dev):
        return remote(cs.at[stage], cr.at[i], cs_s.at[i], cs_r.at[i], dev)

    pl.semaphore_wait(barrier, len(greet))
    cs_copies = [cs_copy(0, i, d) for i, d in enumerate(plane)]
    cs_copies += [cs_copy(1, 6 + o, xdev(o)) for o in (1, 2, 3)]
    for copy in cs_copies[:7]:
        copy.start()
    along = z >= 3 - 2 * zl

    @pl.when(along)
    def _():
        for t in range(T):
            e_copy(t).start()

    for copy in cs_copies[:7]:
        copy.wait_recv()
    cs[1] = ((cs[0] + cr[0]) + (cr[1] + cr[2])) + ((cr[3] + cr[4]) + (cr[5] + cr[6]))
    for copy in cs_copies[7:]:
        copy.start()

    @pl.when(jnp.logical_not(along))
    def _():
        for t in range(2):
            e_copy(t).start()

    @pl.when(c == 0)
    def _():
        x_copy(0).start()

    @pl.when(jnp.logical_not(along))
    def _():
        for t in range(2, T):
            e_copy(t).start()

    @pl.when(c == 0)
    def _():
        for t in range(1, T):
            x_copy(t).start()

    @pl.when(c == 1)
    def _():
        for t in range(T):
            ce_copy(t, a).start()

    for copy in cs_copies[7:]:
        copy.wait_recv()
    pixel_mean = ((cs[1] + cr[7]) + (cr[8] + cr[9])) / total_frames
    inv8 = 1.0 / pixel_mean
    for i in range(8):
        winv[0:1, i * width:(i + 1) * width] = inv8[i:i + 1, :]

    def scaled(v):
        w = winv[0:1, :] * winv[0:1, :]
        return (v.astype(F32) * w).astype(BF16)

    early = 4 - 2 * zl
    late = 2 + 2 * zl
    m_self, m_ex, m_early, m_late, m_far = 0, 1, 2, 2 + T, 2 + 2 * T
    messages = [(0, 0, 1, 0, BS), (1, 1, 1, 0, BS)]
    messages += [(m_early + t, early, 2, t * CR, CR) for t in range(T)]
    messages += [(m_late + t, late, 2, t * CR, CR) for t in range(T)]

    def y_copy(m, o):
        dst = lax.rem(y + o, 4)
        _, s0, ns, c0, nc = messages[m]
        return remote(
            ys.at[pl.ds(s0, ns), :, dst, :, pl.ds(c0, nc)], yr.at[o - 1, pl.ds(s0, ns), :, :, pl.ds(c0, nc)],
            ys_s.at[m, o - 1], ys_r.at[m, o - 1], ydev(o))

    def far_rows(t, o):
        dst = lax.rem(y + o, 4)
        return remote(
            ys.at[pl.ds(6, 2), :, dst, pl.ds(t * CS, CS), :], yr.at[o - 1, pl.ds(6, 2), :, pl.ds(t * CS, CS), :],
            ys_s.at[m_far + t, o - 1], ys_r.at[m_far + t, o - 1], ydev(o))

    def far_cols(t, o):
        dst = lax.rem(y + o, 4)
        return remote(
            ys.at[pl.ds(6, 2), :, dst, :, pl.ds(t * CR, CR)], yr.at[o - 1, pl.ds(6, 2), :, :, pl.ds(t * CR, CR)],
            ys_s.at[m_far + t, o - 1], ys_r.at[m_far + t, o - 1], ydev(o))

    def y_start(m):
        for o in (2, 1, 3):
            y_copy(m, o).start()

    def z_copy(m):
        _, s0, ns, c0, nc = messages[m]
        return remote(zs.at[pl.ds(s0, ns), :, pl.ds(c0, nc)], zr.at[pl.ds(s0, ns), :, pl.ds(c0, nc)],
                      zs_s.at[m], zs_r.at[m], zpartner)

    def total(s, h, r, q):
        return (ys[s, h, y, r, q] + yr[0, s, h, r, q]) + (yr[1, s, h, r, q] + yr[2, s, h, r, q])

    def z_start(m):
        _, s0, ns, c0, nc = messages[m]
        for o in (1, 2, 3):
            y_copy(m, o).wait_recv()
        cols = pl.ds(c0, nc)
        for i in range(ns):
            zs[s0 + i, :, cols] = total(s0 + i, 1 - zl, slice(None), cols)
        z_copy(m).start()
        for i in range(ns):
            zo[s0 + i, :, cols] = total(s0 + i, zl, slice(None), cols)

    def home_copy(t, h, r, q):
        return remote(hs.at[h, :, r, q], hb.at[zl, :, r, q], hs_s.at[t, h], hb_r.at[zl, t], homes[h])

    def far_home(t):
        @pl.when(zl == 0)
        def _():
            r, q = pl.ds(t * CS, CS), pl.ds(0, BS)
            for o in (1, 2, 3):
                far_rows(t, o).wait_recv()
            for h in range(2):
                for j in range(2):
                    hs[h, j, r, :] = total(6 + j, h, r, q)
                home_copy(t, h, r, q).start()

        @pl.when(zl == 1)
        def _():
            r, q = pl.ds(0, SH), pl.ds(t * CR, CR)
            for o in (1, 2, 3):
                far_cols(t, o).wait_recv()
            for h in range(2):
                for j in range(2):
                    hs[h, j, :, q] = total(6 + j, h, r, q)
                home_copy(t, h, r, q).start()

    def pair_product(left, e, s0, t):
        right = rv[e, t].reshape(2 * CR, pix)
        for h in range(2):
            prod = nt_dot(left[4 * h:4 * h + 4].reshape(4 * SH, pix), right)
            for j in range(2):
                ys[s0 + j, h, :, :, t * CR:(t + 1) * CR] = prod[:, j * CR:(j + 1) * CR].reshape(4, SH, CR)

    def single_product(left, right, s):
        for h in range(2):
            for q in range(2):
                prod = nt_dot(left[4 * h:4 * h + 4].reshape(4 * SH, pix), right[4 * q:4 * q + 4].reshape(4 * SH, pix))
                ys[s, h, :, :, q * 256:(q + 1) * 256] = prod.reshape(4, SH, 256)

    def far_product(t):
        @pl.when(zl == 0)
        def _():
            lw[...] = scaled(rv[1, t, c].reshape(CR, pix))
            for q in range(T):
                prod = nt_dot(lw[...], rv[0, q].reshape(2 * CR, pix))
                for j in range(2):
                    ys[6 + j, :, :, t * CS:(t + 1) * CS, q * CR:(q + 1) * CR] = (
                        prod[:, j * CR:(j + 1) * CR].reshape(2, 4, CS, CR))
            for o in (2, 1, 3):
                far_rows(t, o).start()

        @pl.when(zl == 1)
        def _():
            pair_product(nw, 1, 6, t)
            for o in (2, 1, 3):
                far_cols(t, o).start()

    def arrive_early(t):
        e_copy(t).wait_recv()
        c_copy(0, t).start()

    def step_early(t):
        c_copy(0, t).wait_recv()
        pair_product(aw, 0, early, t)
        y_start(m_early + t)

        @pl.when(zl == 1)
        def _():
            nw[:, t * CS:(t + 1) * CS, :] = scaled(rv[0, t, c])

    forward = (c == 0) & (z <= 2 * zl)

    def send_late(t):
        @pl.when(forward)
        def _():
            x_copy(t).wait_recv()
            l_copy(t, ap, zdev(3 - 2 * zl)).start()

        @pl.when(jnp.logical_not(forward))
        def _():
            l_copy(t, a, kdev(15 - 2 * zl)).start()

    def send_extra(t):
        @pl.when(c == 0)
        def _():
            @pl.when(jnp.logical_not(forward))
            def _():
                x_copy(t).wait_recv()

            ce_copy(t, ap).start()

    def arrive_late(t):
        l_copy(t, a, core).wait_recv()
        c_copy(1, t).start()

    def step_late(t):
        c_copy(1, t).wait_recv()
        pair_product(aw, 1, late, t)
        y_start(m_late + t)
        far_product(t)

    for q in range(4):
        aw[2 * q:2 * q + 2] = scaled(fr[q * rows:(q + 1) * rows, :] - dk).reshape(2, SH, pix)
    inv = winv[0:1, :]
    hi = inv.astype(BF16).astype(F32)
    row = lax.broadcasted_iota(jnp.int32, (16, pix), 0)
    mix = jnp.where(row == 0, hi, jnp.where(row == 1, inv - hi, 0.0)).astype(BF16)
    fsum = jnp.sum(nt_dot(mix, a[...].reshape(BS, pix)), axis=0, keepdims=True)
    fs[0] = jnp.broadcast_to(fsum, (8, BS))

    def fy_copy(o):
        return remote(fs.at[0], fy.at[o - 1], fy_s.at[o - 1], fy_r.at[o - 1], ydev(o))

    fz_copy = remote(fs.at[1], fz, fz_s.at[0], fz_r.at[0], zpartner)

    def fm_copy(d):
        return remote(fmr.at[0], fmr.at[d], fm_s.at[d], fm_r.at[d], fwrap(-d))

    for o in (1, 2, 3):
        fy_copy(o).start()
    single_product(aw, a, 0)
    y_start(m_self)
    for o in (1, 2, 3):
        fy_copy(o).wait_recv()
    fs[1] = (fs[0] + fy[0]) + (fy[1] + fy[2])
    fz_copy.start()

    arrive_early(0)
    step_early(0)
    arrive_early(1)
    z_start(m_self)
    step_early(1)
    arrive_early(2)
    send_late(0)
    z_start(m_early)
    step_early(2)
    send_late(1)
    arrive_early(3)
    send_late(2)
    send_late(3)
    z_start(m_early + 1)
    step_early(3)
    for t in range(T):
        send_extra(t)
    fz_copy.wait_recv()
    fmr[0] = (fs[1] + fz[...]) / total_pix
    for d in range(1, BAND):
        fm_copy(d).start()
    for t in range(T):
        ce_copy(t, a).wait_recv()
    single_product(aw, ex, 1)
    y_start(m_ex)
    z_start(m_early + 2)
    arrive_late(0)
    z_start(m_early + 3)
    step_late(0)
    z_start(m_ex)
    arrive_late(1)
    z_start(m_late)
    step_late(1)
    far_home(0)
    arrive_late(2)
    z_start(m_late + 1)
    step_late(2)
    far_home(1)

    for d in range(1, BAND):
        fm_copy(d).wait_recv()
    fcol[...] = jnp.transpose(jnp.broadcast_to(fmr[0, 0:1, :], (128, BS)))
    left = 1.0 / (fcol[pl.ds(pl.multiple_of(p * SH, SH), SH), :] * total_pix)
    left = jnp.concatenate([left] * (BS // 128), axis=1)

    def put(lag, v):
        v = v * left * (1.0 / fmr[lag, 0:1, :])
        out[:, lag, :] = jnp.where(f + lag < nf, v, 0.0)

    z_copy(m_self).wait_recv()
    put(0, zo[0] + zr[0])
    z_copy(m_ex).wait_recv()

    @pl.when(c == 0)
    def _():
        put(1, zo[1] + zr[1])

    @pl.when(c == 1)
    def _():
        put(7, zo[1] + zr[1])

    arrive_late(3)
    z_start(m_late + 2)
    step_late(3)
    far_home(2)
    z_start(m_late + 3)
    far_home(3)
    for t in range(T):
        z_copy(m_early + t).wait_recv()
        z_copy(m_late + t).wait_recv()

    def put_pairs(base):
        for j in range(2):
            put(base[0] + j, natural(zo[2 + j] + zr[2 + j]))
            put(base[1] + j, natural(zo[4 + j] + zr[4 + j]))

    @pl.when(c == 0)
    def _():
        put_pairs((2, 6))

    @pl.when(c == 1)
    def _():
        put_pairs((1, 5))

    for t in range(T):
        for w in range(2):
            remote(hs.at[0, :, :, pl.ds(0, CR)], hb.at[w, :, :, pl.ds(0, CR)], hs_s.at[t, 0], hb_r.at[w, t],
                   homes[0]).wait_recv()

    def put_far(base):
        for j in range(2):
            put(base + j, natural(hb[0, j] + hb[1, j]))

    @pl.when(c == 0)
    def _():
        put_far(4)

    @pl.when(c == 1)
    def _():
        put_far(3)

    @pl.when(c == 0)
    def _():
        for t in range(T):
            x_copy(t).wait_send()

    for t in range(T):
        e_copy(t).wait_send()
        l_copy(t, a, core).wait_send()
        ce_copy(t, a).wait_send()
        for e in range(2):
            c_copy(e, t).wait_send()
        for h in range(2):
            home_copy(t, h, pl.ds(0, SH), pl.ds(0, CR)).wait_send()
        for o in (1, 2, 3):
            far_cols(t, o).wait_send()
    for copy in cs_copies:
        copy.wait_send()
    for o in (1, 2, 3):
        fy_copy(o).wait_send()
    fz_copy.wait_send()
    for d in range(1, BAND):
        fm_copy(d).wait_send()
    for m in range(len(messages)):
        for o in (1, 2, 3):
            y_copy(m, o).wait_send()
        z_copy(m).wait_send()


def on_device(frames, dark):
    n, pix = frames.shape
    total_frames = n * lax.axis_size("frame")
    total_pix = pix * lax.axis_size("pix")
    nm = 2 + 3 * T
    nz = 2 + 2 * T
    dma = pltpu.SemaphoreType.DMA
    vm = pltpu.VMEM
    block = (8, SH, pix)
    out = pl.pallas_call(
        functools.partial(kernel, float(total_frames), float(total_pix)),
        out_shape=jax.ShapeDtypeStruct((SH, BAND, BS), F32),
        in_specs=[pl.BlockSpec(memory_space=pl.ANY), pl.BlockSpec(memory_space=pltpu.VMEM)],
        out_specs=pl.BlockSpec(memory_space=pltpu.VMEM),
        scratch_shapes=[
            vm((BS, pix), F32), vm(block, BF16), vm(block, BF16), vm(block, BF16), vm(block, BF16),
            vm((2, T, 2, 8, CS, pix), BF16), vm(block, BF16), vm((CR, pix), BF16),
            vm((8, 2, 4, SH, BS), F32), vm((3, 8, 2, SH, BS), F32),
            vm((6, SH, BS), F32), vm((6, SH, BS), F32), vm((6, SH, BS), F32),
            vm((2, 2, SH, BS), F32), vm((2, 2, SH, BS), F32),
            vm((2, 8, pix // 8), F32), vm((10, 8, pix // 8), F32), vm((8, pix), F32),
            vm((2, 8, BS), F32), vm((3, 8, BS), F32), vm((8, BS), F32), vm((BAND, 8, BS), F32), vm((BS, 128), F32),
            dma((4,)),
            dma((T,)), dma((T,)), dma((T,)), dma((T,)), dma((T,)), dma((T,)),
            dma((T,)), dma((T,)), dma((2, T)), dma((2, T)),
            dma((nm, 3)), dma((nm, 3)), dma((nz,)), dma((nz,)), dma((T, 2)), dma((2, T)),
            dma((10,)), dma((10,)), dma((3,)), dma((3,)), dma((1,)), dma((1,)), dma((BAND,)), dma((BAND,)),
        ],
        compiler_params=pltpu.CompilerParams(
            collective_id=0, has_side_effects=True, vmem_limit_bytes=56 * 1024 * 1024),
        cost_estimate=pl.CostEstimate(flops=2 * 8 * BS * BS * pix, bytes_accessed=6 * BS * pix, transcendentals=0),
    )(frames, dark.reshape(1, pix))
    return out.reshape(SH, 1, BAND, BS)


def solution(mesh):
    return jax.shard_map(
        on_device,
        mesh=mesh,
        in_specs=(P("frame", "pix"), P("pix")),
        out_specs=P("pix", "frame", None, None),
        check_vma=False,
    )
```

time: 571 us -> 187 us (0.33)
  waiting for transfers between devices: 368 us -> 0 us
  Pallas kernels: 0 us -> 184 us
  blocking collectives: 120 us -> 0 us
  starting transfers between devices: 19.5 us -> 0 us
  local copies, waits for them, and re-layouts: 21.6 us -> 2.26 us
  other arithmetic: 16.1 us -> 0 us
  between operations: 13.5 us -> 0.01 us
  matrix products: 11.7 us -> 0 us
    ppermute x7 -> x0, waiting for transfers between devices: 301 us -> none  [from_behind(): return lax.ppermute(block, axis, route)]
    pallas_call x0 -> x1, Pallas kernels: none -> 184 us  [on_device(): pl.pallas_call(functools.partial(kernel, float(total_frames), float(total...]
    psum x2 -> x0, blocking collectives: 120 us -> none  [the longest x1 74.4 us: on_device(): pixel_mean = lax.psum(jnp.sum(signal, axis=0), 'frame') / total_frames]
    reduce_scatter x1 -> x0, waiting for transfers between devices: 67.1 us -> none  [on_device(): lax.psum_scatter(jnp.stack(products_list, axis=1), 'pix', scatter_dimensi...]
    ppermute x7 -> x0, starting transfers between devices: 19.5 us -> none  [from_behind(): return lax.ppermute(block, axis, route)]
    unnamed x7 -> x1, local copies, waits for them, and re-layouts: 20.2 us -> 2.26 us
    dot_general x1 -> x0, matrix products: 11.7 us -> none  [on_device(): lax.dot_general(normalized, extended, (((1,), (1,)), ((), ())), preferred...]
    reduce_sum x2 -> x0, other arithmetic: 9.4 us -> none  [the longest x1 6.83 us: on_device(): jnp.sum(extended, axis=1, dtype=jnp.float32)]
  transfers between devices with their start and end apart: 8 -> 0, of which waited for: 8 -> 0; matrix products, arithmetic and copies ran while one was open for 3% -> 0% of each run, Pallas kernels for 0% -> 0%
where the time goes in v2:
time: 187 us; the launch traced here: 186 us
  Pallas kernels  184 us (98%)
  local copies, waits for them, and re-layouts  2.26 us (1%)
    pallas_call x1, Pallas kernels, on_device(): pl.pallas_call(functools.partial(kernel, float(total_frames), float(total...  184 us

profile of v2, /device:TPU:1, one launch (start us, length us, event | category | flops | bytes accessed | tf_op | source)
XLA Modules:
  0.0 186.3 jit_solution(2587163604184736617)
XLA Ops:
  0.0 184.0 %shard_map.28 = f32[64,8,512]{2,1,0:T(8,128)} custom-call(f32[512,2048]{1,0:T(8,128)} %frames.1, f32[1,2048]{1,0:T(1,128)} %bitcast.5), custom_call_target="tpu_custom_call" | custom-call | flops 8589934592 | bytes 6291456 | tf_op jit(solution)/shard_map/pallas_call | solution.py:502
  184.0 2.3 %copy.5 = f32[64,1,8,512]{3,2,1,0:T(8,128)} copy(f32[64,1,8,512]{3,2,1,0:T(8,128)} %bitcast.4) | data formatting | bytes 2097152

commit v3 on v2

--- a/solution.py
+++ b/solution.py
@@ -152,23 +152,13 @@
     for copy in cs_copies[7:]:
         copy.start()
 
-    @pl.when(jnp.logical_not(along))
-    def _():
-        for t in range(2):
+    for t in range(T):
+        @pl.when(jnp.logical_not(along))
+        def _():
             e_copy(t).start()
 
-    @pl.when(c == 0)
-    def _():
-        x_copy(0).start()
-
-    @pl.when(jnp.logical_not(along))
-    def _():
-        for t in range(2, T):
-            e_copy(t).start()
-
-    @pl.when(c == 0)
-    def _():
-        for t in range(1, T):
+        @pl.when(c == 0)
+        def _():
             x_copy(t).start()
 
     @pl.when(c == 1)
@@ -225,21 +215,24 @@
     def total(s, h, r, q):
         return (ys[s, h, y, r, q] + yr[0, s, h, r, q]) + (yr[1, s, h, r, q] + yr[2, s, h, r, q])
 
-    def z_start(m):
+    def z_sum(m):
         _, s0, ns, c0, nc = messages[m]
         for o in (1, 2, 3):
             y_copy(m, o).wait_recv()
         cols = pl.ds(c0, nc)
         for i in range(ns):
             zs[s0 + i, :, cols] = total(s0 + i, 1 - zl, slice(None), cols)
-        z_copy(m).start()
         for i in range(ns):
             zo[s0 + i, :, cols] = total(s0 + i, zl, slice(None), cols)
 
+    def z_start(m):
+        z_sum(m)
+        z_copy(m).start()
+
     def home_copy(t, h, r, q):
         return remote(hs.at[h, :, r, q], hb.at[zl, :, r, q], hs_s.at[t, h], hb_r.at[zl, t], homes[h])
 
-    def far_home(t):
+    def far_sum(t):
         @pl.when(zl == 0)
         def _():
             r, q = pl.ds(t * CS, CS), pl.ds(0, BS)
@@ -248,7 +241,6 @@
             for h in range(2):
                 for j in range(2):
                     hs[h, j, r, :] = total(6 + j, h, r, q)
-                home_copy(t, h, r, q).start()
 
         @pl.when(zl == 1)
         def _():
@@ -258,7 +250,21 @@
             for h in range(2):
                 for j in range(2):
                     hs[h, j, :, q] = total(6 + j, h, r, q)
-                home_copy(t, h, r, q).start()
+
+    def far_send(t):
+        @pl.when(zl == 0)
+        def _():
+            for h in range(2):
+                home_copy(t, h, pl.ds(t * CS, CS), pl.ds(0, BS)).start()
+
+        @pl.when(zl == 1)
+        def _():
+            for h in range(2):
+                home_copy(t, h, pl.ds(0, SH), pl.ds(t * CR, CR)).start()
+
+    def far_home(t):
+        far_sum(t)
+        far_send(t)
 
     def pair_product(left, e, s0, t):
         right = rv[e, t].reshape(2 * CR, pix)
@@ -306,15 +312,17 @@
 
     forward = (c == 0) & (z <= 2 * zl)
 
-    def send_late(t):
+    def send_late():
+        @pl.when(jnp.logical_not(forward))
+        def _():
+            for t in range(T):
+                l_copy(t, a, kdev(15 - 2 * zl)).start()
+
+    def forward_late(t):
         @pl.when(forward)
         def _():
             x_copy(t).wait_recv()
             l_copy(t, ap, zdev(3 - 2 * zl)).start()
-
-        @pl.when(jnp.logical_not(forward))
-        def _():
-            l_copy(t, a, kdev(15 - 2 * zl)).start()
 
     def send_extra(t):
         @pl.when(c == 0)
@@ -361,44 +369,45 @@
     fs[1] = (fs[0] + fy[0]) + (fy[1] + fy[2])
     fz_copy.start()
 
+    def step_extra(core_index):
+        @pl.when(c == core_index)
+        def _():
+            for t in range(T):
+                ce_copy(t, a).wait_recv()
+            single_product(aw, ex, 1)
+            y_start(m_ex)
+
     arrive_early(0)
     step_early(0)
+    step_extra(0)
     arrive_early(1)
-    z_start(m_self)
     step_early(1)
     arrive_early(2)
-    send_late(0)
-    z_start(m_early)
+    send_late()
     step_early(2)
-    send_late(1)
+    forward_late(0)
+    forward_late(1)
     arrive_early(3)
-    send_late(2)
-    send_late(3)
-    z_start(m_early + 1)
+    forward_late(2)
     step_early(3)
-    for t in range(T):
-        send_extra(t)
+    forward_late(3)
     fz_copy.wait_recv()
     fmr[0] = (fs[1] + fz[...]) / total_pix
     for d in range(1, BAND):
         fm_copy(d).start()
+    arrive_late(0)
+    step_late(0)
     for t in range(T):
-        ce_copy(t, a).wait_recv()
-    single_product(aw, ex, 1)
-    y_start(m_ex)
+        send_extra(t)
+    arrive_late(1)
+    step_late(1)
+    step_extra(1)
+    z_start(m_self)
+    z_start(m_early)
+    arrive_late(2)
+    step_late(2)
+    z_start(m_early + 1)
     z_start(m_early + 2)
-    arrive_late(0)
-    z_start(m_early + 3)
-    step_late(0)
-    z_start(m_ex)
-    arrive_late(1)
-    z_start(m_late)
-    step_late(1)
-    far_home(0)
-    arrive_late(2)
-    z_start(m_late + 1)
-    step_late(2)
-    far_home(1)
 
     for d in range(1, BAND):
         fm_copy(d).wait_recv()
@@ -410,8 +419,18 @@
         v = v * left * (1.0 / fmr[lag, 0:1, :])
         out[:, lag, :] = jnp.where(f + lag < nf, v, 0.0)
 
+    arrive_late(3)
+    step_late(3)
+    z_start(m_early + 3)
+    z_start(m_late)
+    far_home(0)
+    z_start(m_late + 1)
+    far_home(1)
+    z_start(m_ex)
     z_copy(m_self).wait_recv()
     put(0, zo[0] + zr[0])
+    z_start(m_late + 2)
+    far_home(2)
     z_copy(m_ex).wait_recv()
 
     @pl.when(c == 0)
@@ -422,10 +441,6 @@
     def _():
         put(7, zo[1] + zr[1])
 
-    arrive_late(3)
-    z_start(m_late + 2)
-    step_late(3)
-    far_home(2)
     z_start(m_late + 3)
     far_home(3)
     for t in range(T):

time: 187 us -> 180 us (0.963)
  Pallas kernels: 184 us -> 178 us
    pallas_call x1, Pallas kernels: 184 us -> 178 us  [on_device(): pl.pallas_call(functools.partial(kernel, float(total_frames), float(total...]
where the time goes in v3:
time: 180 us
  Pallas kernels  178 us (99%)
  local copies, waits for them, and re-layouts  2.26 us (1%)
    pallas_call x1, Pallas kernels, on_device(): pl.pallas_call(functools.partial(kernel, float(total_frames), float(total...  178 us

profile of v3, /device:TPU:1, one launch (start us, length us, event | category | flops | bytes accessed | tf_op | source)
XLA Modules:
  0.0 180.0 jit_solution(609524585378380148)
XLA Ops:
  0.0 177.7 %shard_map.28 = f32[64,8,512]{2,1,0:T(8,128)} custom-call(f32[512,2048]{1,0:T(8,128)} %frames.1, f32[1,2048]{1,0:T(1,128)} %bitcast.5), custom_call_target="tpu_custom_call" | custom-call | flops 8589934592 | bytes 6291456 | tf_op jit(solution)/shard_map/pallas_call | solution.py:517
  177.7 2.3 %copy.5 = f32[64,1,8,512]{3,2,1,0:T(8,128)} copy(f32[64,1,8,512]{3,2,1,0:T(8,128)} %bitcast.4) | data formatting | bytes 2097152

commit v4 on v3

--- a/solution.py
+++ b/solution.py
@@ -339,9 +339,9 @@
 
     def step_late(t):
         c_copy(1, t).wait_recv()
+        far_product(t)
         pair_product(aw, 1, late, t)
         y_start(m_late + t)
-        far_product(t)
 
     for q in range(4):
         aw[2 * q:2 * q + 2] = scaled(fr[q * rows:(q + 1) * rows, :] - dk).reshape(2, SH, pix)
@@ -422,15 +422,15 @@
     arrive_late(3)
     step_late(3)
     z_start(m_early + 3)
+    far_home(0)
     z_start(m_late)
-    far_home(0)
+    far_home(1)
     z_start(m_late + 1)
-    far_home(1)
     z_start(m_ex)
     z_copy(m_self).wait_recv()
     put(0, zo[0] + zr[0])
+    far_home(2)
     z_start(m_late + 2)
-    far_home(2)
     z_copy(m_ex).wait_recv()
 
     @pl.when(c == 0)
@@ -441,8 +441,8 @@
     def _():
         put(7, zo[1] + zr[1])
 
+    far_home(3)
     z_start(m_late + 3)
-    far_home(3)
     for t in range(T):
         z_copy(m_early + t).wait_recv()
         z_copy(m_late + t).wait_recv()

time: 180 us -> 177 us (0.983)
  Pallas kernels: 178 us -> 175 us
    pallas_call x1, Pallas kernels: 178 us -> 175 us  [on_device(): pl.pallas_call(functools.partial(kernel, float(total_frames), float(total...]
where the time goes in v4:
time: 177 us
  Pallas kernels  175 us (99%)
  local copies, waits for them, and re-layouts  2.26 us (1%)
    pallas_call x1, Pallas kernels, on_device(): pl.pallas_call(functools.partial(kernel, float(total_frames), float(total...  175 us

profile of v4, /device:TPU:1, one launch (start us, length us, event | category | flops | bytes accessed | tf_op | source)
XLA Modules:
  0.0 177.2 jit_solution(16352840378068847836)
XLA Ops:
  0.0 174.9 %shard_map.28 = f32[64,8,512]{2,1,0:T(8,128)} custom-call(f32[512,2048]{1,0:T(8,128)} %frames.1, f32[1,2048]{1,0:T(1,128)} %bitcast.5), custom_call_target="tpu_custom_call" | custom-call | flops 8589934592 | bytes 6291456 | tf_op jit(solution)/shard_map/pallas_call | solution.py:517
  174.9 2.3 %copy.5 = f32[64,1,8,512]{3,2,1,0:T(8,128)} copy(f32[64,1,8,512]{3,2,1,0:T(8,128)} %bitcast.4) | data formatting | bytes 2097152
